TPU v7x, 256 devices: a whole 4x4x8 slice. The times are simulated.
256 devices in a mesh: row: 64 (over y, x_hi, z), ch: 4 (over x_lo, core).
Axes of the slice: x: 4 (x_hi: 2, x_lo: 2; x = x_hi * 2 + x_lo), y: 4, z: 8, core: 2. Of those that a mesh axis runs over, the one named last changes fastest.
Arguments:
- pair_field: bfloat16 [128, 512, 512], P('ch', 'row'), may hold values from -25 to 25
- input_gain: float32 [128], replicated, may hold values from 0.5 to 1.5
- input_bias: float32 [128], replicated, may hold values from -1.2 to 1.2
- left_weight: bfloat16 [128, 128], P(None, 'ch'), may hold values from -0.5 to 0.5
- left_gate: bfloat16 [128, 128], P(None, 'ch'), may hold values from -0.5 to 0.5
- right_weight: bfloat16 [128, 128], P(None, 'ch'), may hold values from -0.5 to 0.5
- right_gate: bfloat16 [128, 128], P(None, 'ch'), may hold values from -0.5 to 0.5
- gate_weight: bfloat16 [128, 128], P(None, 'ch'), may hold values from -0.5 to 0.5
- output_gain: float32 [128], replicated, may hold values from 0.5 to 1.5
- output_bias: float32 [128], replicated, may hold values from -1.2 to 1.2
- final_weight: bfloat16 [128, 128], P(None, 'ch'), may hold values from -0.5 to 0.5
Outputs:
- transposed: bfloat16 [128, 512, 512], P('ch', 'row')
All inputs are finite; a program needn't handle non-finite values.
Results may differ from a plain program's by a relative error of at most 0.012.
Values may be sent and summed in bfloat16 or wider, within the bound.
No kernel may reach another device: no remote copies, remote signals or barrier semaphores. Data moves between devices by JAX's collectives and lax.ppermute only.
A program may use at most 64 MiB of HBM per device.

v0:
```python
import jax
import jax.numpy as jnp
from jax import lax
from jax.sharding import PartitionSpec as P

epsilon = 1e-05


def layer_norm(values, gain, bias):
    average = jnp.mean(values, axis=0, keepdims=True)
    centred = values - average
    variance = jnp.mean(centred * centred, axis=0, keepdims=True)
    return centred * lax.rsqrt(variance + epsilon) * gain[:, None, None] + bias[:, None, None]


def project(normed, weight):
    flat_field = normed.reshape(normed.shape[0], normed.shape[1] * normed.shape[2])
    result = jnp.dot(jnp.transpose(weight), flat_field, preferred_element_type=jnp.float32)
    return result.reshape(weight.shape[1], normed.shape[1], normed.shape[2])


def contract(first, second, form):
    return jnp.einsum(
        form, first.astype(jnp.float32), second.astype(jnp.float32), precision=lax.Precision.HIGHEST
    )


def body(
    pair_field,
    input_gain,
    input_bias,
    left_weight,
    left_gate,
    right_weight,
    right_gate,
    gate_weight,
    output_gain,
    output_bias,
    final_weight,
):
    gathered = lax.all_gather(pair_field, "ch", axis=0, tiled=True)
    normed = layer_norm(gathered.astype(jnp.float32), input_gain, input_bias).astype(jnp.bfloat16)
    left_factor = (
        jax.nn.sigmoid(project(normed, left_gate)) * project(normed, left_weight)
    ).astype(jnp.bfloat16)
    right_factor = (
        jax.nn.sigmoid(project(normed, right_gate)) * project(normed, right_weight)
    ).astype(jnp.bfloat16)
    gating = jax.nn.sigmoid(project(normed, gate_weight)).astype(jnp.bfloat16)
    product = contract(
        left_factor, lax.all_gather(right_factor, "row", axis=1, tiled=True), "cik,cjk->cij"
    )
    hidden_all = lax.all_gather(product.astype(jnp.bfloat16), "ch", axis=0, tiled=True)
    hidden_normed = layer_norm(hidden_all.astype(jnp.float32), output_gain, output_bias).astype(
        jnp.bfloat16
    )
    update = (gating.astype(jnp.float32) * project(hidden_normed, final_weight)).astype(
        jnp.bfloat16
    )
    return lax.all_to_all(
        jnp.swapaxes(update, 1, 2), "row", split_axis=1, concat_axis=2, tiled=True
    )


def solution(mesh):
    placed = (
        P("ch", "row", None),
        P(),
        P(),
        P(None, "ch"),
        P(None, "ch"),
        P(None, "ch"),
        P(None, "ch"),
        P(None, "ch"),
        P(),
        P(),
        P(None, "ch"),
    )
    return jax.shard_map(
        body, mesh=mesh, in_specs=placed, out_specs=P("ch", "row", None), check_vma=False
    )
```

profile of v0, /device:TPU:1, one launch (start us, length us, event | category | flops | bytes accessed | tf_op | source)
XLA Modules:
  0.0 340.5 jit_solution(7408528371137574967)
XLA Ops:
  6.5 0.7 all-gather.4.cloned.1.call-update
  7.3 0.0 all-gather.6.cloned.1.call-start
  7.3 29.3 %all-gather.4.cloned.1.call-done = bf16[128,8,512]{2,1,0:T(8,128)(2,1)} async-done(((bf16[32,8,512]{2,1,0:T(8,128)(2,1)}), bf16[128,8,512]{2,1,0:T(8,128)(2,1)}) %all-gather.4.cloned.1.call-update) | async-done | bytes 1048592 | tf_op jit(solution)/shard_map/all_gather | solution.py:41
  36.7 1.5 convert_reduce_fusion.1
  38.2 1.6 fusion.22
  39.8 0.4 fusion.25
  40.2 0.4 copy.19
  40.6 0.3 fusion.2
  40.9 0.3 fusion.12
  41.2 0.8 copy.21
  42.0 0.0 all-gather.6.cloned.1.call-update
  42.0 0.0 all-gather.8.cloned.1.call-start
  42.1 0.3 fusion.5
  42.4 0.3 fusion.11
  42.7 0.1 copy.20
  42.8 223.6 %all-gather.6.cloned.1.call-done = bf16[32,512,512]{2,1,0:T(8,128)(2,1)} async-done(((bf16[32,8,512]{2,1,0:T(8,128)(2,1)}), bf16[32,512,512]{2,1,0:T(8,128)(2,1)}) %all-gather.6.cloned.1.call-update) | async-done | bytes 16777232 | tf_op jit(solution)/shard_map/all_gather | solution.py:51
  266.4 10.9 %convolution_convert_fusion = bf16[32,8,512]{2,1,0:T(8,128)(2,1)} fusion(bf16[32,8,512]{2,1,0:T(8,128)(2,1)S(1)} %bitcast.48, bf16[32,512,512]{2,1,0:T(8,128)(2,1)} %all-gather.6.cloned.1.call-done), kind=kOutput, calls=%fused_computation.36 | convolution fusion | flops 134348800 | bytes 17301504 | tf_op jit(solution)/shard_map/cik,cjk->cij/dot_general | solution.py:23
  277.3 0.3 fusion.10
  277.6 22.2 %all-gather.8.cloned.1.call-done = bf16[128,8,512]{2,1,0:T(8,128)(2,1)} async-done(((bf16[32,8,512]{2,1,0:T(8,128)(2,1)}), bf16[128,8,512]{2,1,0:T(8,128)(2,1)}) %all-gather.8.cloned.1.call-update) | async-done | bytes 1048592 | tf_op jit(solution)/shard_map/all_gather | solution.py:53
  299.9 1.5 convert_reduce_fusion
  301.4 1.6 fusion.18
  303.0 0.4 fusion.21
  303.4 0.4 copy.22
  303.8 0.3 fusion.13
  304.1 0.1 copy.23
  304.2 0.8 copy.16
  305.1 0.1 bitcast_bitcast_fusion
  305.1 1.0 reshape.87
  306.1 25.8 %all_to_all.18 = bf16[64,2,1024]{2,1,0:T(2,128)(2,1)S(1)} all-to-all(bf16[64,2,1024]{2,1,0:T(2,128)(2,1)S(1)} %reshape.87), channel_id=1, replica_groups=mesh['row'=64,'ch'=4] {'row'}, dimensions={0} | all-to-all | bytes 524288 | tf_op jit(solution)/shard_map/all_to_all | solution.py:60
  332.0 0.5 reshape.88
  332.5 0.2 copy.25
  332.7 1.3 copy.18
  (30 shorter events, 0.1 us)
Async XLA Ops:
  6.5 34.1 %copy-start = (bf16[128,32]{0,1:T(8,128)(2,1)S(1)}, bf16[128,32]{0,1:T(8,128)(2,1)}, u32[]{:S(2)}) copy-start(bf16[128,32]{0,1:T(8,128)(2,1)} %param.17) | copy-start | bytes 24580
  6.5 33.2 %copy-start.6 = (f32[128]{0:T(128)S(1)}, f32[128]{0:T(128)}, u32[]{:S(2)}) copy-start(f32[128]{0:T(128)} %param.13) | copy-start | bytes 1540
  6.5 33.2 %copy-start.7 = (f32[128]{0:T(128)S(1)}, f32[128]{0:T(128)}, u32[]{:S(2)}) copy-start(f32[128]{0:T(128)} %param.12) | copy-start | bytes 1540
  6.5 30.1 %all-gather.4.cloned.1.call-start = ((), (), s32[]{:S(2)}) async-start(), calls=%async_computation.1 | async-start | bytes 1310720 | tf_op jit(solution)/shard_map/all_gather | solution.py:41
  7.3 259.1 %all-gather.6.cloned.1.call-start = ((), (), s32[]{:S(2)}) async-start(), calls=%async_computation.2 | async-start | bytes 17039360 | tf_op jit(solution)/shard_map/all_gather | solution.py:51
  36.7 3.1 copy-start.2
  40.2 0.7 copy-start.3
  40.6 1.5 copy-start.10
  41.2 1.2 copy-start.4
  42.0 257.9 %all-gather.8.cloned.1.call-start = ((), (), s32[]{:S(2)}) async-start(), calls=%async_computation.3 | async-start | bytes 1310720 | tf_op jit(solution)/shard_map/all_gather | solution.py:53
  266.4 11.0 %copy-start.11 = (bf16[128,32]{0,1:T(8,128)(2,1)S(1)}, bf16[128,32]{0,1:T(8,128)(2,1)}, u32[]{:S(2)}) copy-start(bf16[128,32]{0,1:T(8,128)(2,1)} %param.18) | copy-start | bytes 24580
  277.3 25.6 %copy-start.8 = (f32[128]{0:T(128)S(1)}, f32[128]{0:T(128)}, u32[]{:S(2)}) copy-start(f32[128]{0:T(128)} %param.20) | copy-start | bytes 1540
  277.3 25.6 %copy-start.9 = (f32[128]{0:T(128)S(1)}, f32[128]{0:T(128)}, u32[]{:S(2)}) copy-start(f32[128]{0:T(128)} %param.19) | copy-start | bytes 1540
  299.9 3.1 copy-start.1
  303.0 0.8 copy-start.5
Sparse Core Ops, SparseCore 0:
  9.2 27.4 all-gather.3
  42.1 224.1 all-gather.5
  277.4 22.4 all-gather.7
where the time goes:
time: 341 us; the launch traced here: 340 us
  waiting for transfers between devices  276 us (81%)
  blocking collectives  25.8 us (8%)
  between operations  13.4 us (4%)
  matrix products  12.6 us (4%)
  other arithmetic  6.98 us (2%)
  local copies, waits for them, and re-layouts  5.68 us (2%)
    all_gather x1, waiting for transfers between devices, body(): lax.all_gather(right_factor, 'row', axis=1, tiled=True)  224 us
    all_gather x1, waiting for transfers between devices, body(): gathered = lax.all_gather(pair_field, 'ch', axis=0, tiled=True)  29.3 us
    all_to_all x1, blocking collectives, body(): lax.all_to_all(jnp.swapaxes(update, 1, 2), 'row', split_axis=1, concat_ax...  25.8 us
    all_gather x1, waiting for transfers between devices, body(): lax.all_gather(product.astype(jnp.bfloat16), 'ch', axis=0, tiled=True)  22.2 us
    dot_general x1, matrix products, contract(): jnp.einsum(form, first.astype(jnp.float32), second.astype(jnp.float32), p...  10.9 us
  transfers between devices with their start and end apart: 3, of which 3 were waited for; matrix products, arithmetic and copies ran while one was open for 0% of the time, Pallas kernels for 0%

commit v1 on v0

--- a/solution.py
+++ b/solution.py
@@ -48,7 +48,11 @@
     ).astype(jnp.bfloat16)
     gating = jax.nn.sigmoid(project(normed, gate_weight)).astype(jnp.bfloat16)
     product = contract(
-        left_factor, lax.all_gather(right_factor, "row", axis=1, tiled=True), "cik,cjk->cij"
+        left_factor,
+        jnp.concatenate(
+            lax.all_to_all(jnp.stack([right_factor] * lax.axis_size("row")), "row", 0, 0), axis=1
+        ),
+        "cik,cjk->cij",
     )
     hidden_all = lax.all_gather(product.astype(jnp.bfloat16), "ch", axis=0, tiled=True)
     hidden_normed = layer_norm(hidden_all.astype(jnp.float32), output_gain, output_bias).astype(

time: 341 us -> 530 us (1.55)
  waiting for transfers between devices: 276 us -> 448 us
  starting transfers between devices: 0.08 us -> 12.8 us
  local copies, waits for them, and re-layouts: 5.68 us -> 11.3 us
    all_to_all x0 -> x1, waiting for transfers between devices: none -> 377 us  [body(): lax.all_to_all(jnp.stack([right_factor] * lax.axis_size('row')), 'row', 0...]
    all_gather x1 -> x0, waiting for transfers between devices: 224 us -> none  [body(): lax.all_gather(right_factor, 'row', axis=1, tiled=True)]
    all_gather x1, waiting for transfers between devices: 22.2 us -> 40.7 us  [body(): lax.all_gather(product.astype(jnp.bfloat16), 'ch', axis=0, tiled=True)]
    all_to_all x0 -> x1, starting transfers between devices: none -> 12.7 us  [body(): lax.all_to_all(jnp.stack([right_factor] * lax.axis_size('row')), 'row', 0...]
    another operation x0 -> x1, local copies, waits for them, and re-layouts: none -> 6.02 us  [body(): jnp.stack([right_factor] * lax.axis_size('row'))]
where the time goes in v1:
time: 530 us; the launch traced here: 529 us
  waiting for transfers between devices  448 us (85%)
  blocking collectives  25.8 us (5%)
  between operations  13.7 us (3%)
  starting transfers between devices  12.8 us (2%)
  local copies, waits for them, and re-layouts  11.3 us (2%)
  matrix products  10.5 us (2%)
  other arithmetic  6.98 us (1%)
    all_to_all x1, waiting for transfers between devices, body(): lax.all_to_all(jnp.stack([right_factor] * lax.axis_size('row')), 'row', 0...  377 us
    all_gather x1, waiting for transfers between devices, body(): lax.all_gather(product.astype(jnp.bfloat16), 'ch', axis=0, tiled=True)  40.7 us
    all_gather x1, waiting for transfers between devices, body(): gathered = lax.all_gather(pair_field, 'ch', axis=0, tiled=True)  29.4 us
    all_to_all x1, blocking collectives, body(): lax.all_to_all(jnp.swapaxes(update, 1, 2), 'row', split_axis=1, concat_ax...  25.8 us
    all_to_all x1, starting transfers between devices, body(): lax.all_to_all(jnp.stack([right_factor] * lax.axis_size('row')), 'row', 0...  12.7 us
  transfers between devices with their start and end apart: 3, of which 3 were waited for; matrix products, arithmetic and copies ran while one was open for 0% of the time, Pallas kernels for 0%

profile of v1, /device:TPU:1, one launch (start us, length us, event | category | flops | bytes accessed | tf_op | source)
XLA Modules:
  0.0 529.3 jit_solution(1450821578878783103)
XLA Ops:
  6.5 0.7 all-gather.3.cloned.1.call-update
  7.3 29.4 %all-gather.3.cloned.1.call-done = bf16[128,8,512]{2,1,0:T(8,128)(2,1)} async-done(((bf16[32,8,512]{2,1,0:T(8,128)(2,1)}), bf16[128,8,512]{2,1,0:T(8,128)(2,1)}) %all-gather.3.cloned.1.call-update) | async-done | bytes 1048592 | tf_op jit(solution)/shard_map/all_gather | solution.py:41
  36.7 1.5 convert_reduce_fusion.1
  38.2 1.6 fusion.25
  39.8 0.4 fusion.28
  40.2 0.4 copy.20
  40.6 0.3 fusion.5
  40.9 0.3 fusion.15
  41.2 0.1 copy.22
  41.3 6.0 %stack.2 = bf16[64,32,8,512]{3,2,1,0:T(8,128)(2,1)} broadcast(bf16[32,8,512]{2,1,0:T(8,128)(2,1)S(1)} %bitcast.57), dimensions={1,2,3} | broadcast | bytes 17039360 | tf_op jit(solution)/shard_map/stack | solution.py:53
  47.3 12.7 %all-to-all-start = ((bf16[64,32,8,512]{3,2,1,0:T(8,128)(2,1)}), bf16[64,32,8,512]{3,2,1,0:T(8,128)(2,1)}, u32[]{:S(2)}, u32[]{:S(2)}) async-start(bf16[64,32,8,512]{3,2,1,0:T(8,128)(2,1)} %stack.2), calls=%async_computation | async-start | bytes 33554432 | tf_op jit(solution)/shard_map/all_to_all | solution.py:53
  60.1 0.3 fusion.8
  60.4 0.3 copy-done.4
  60.7 0.3 fusion.14
  61.0 0.1 copy.21
  61.1 377.4 %all-to-all-done = bf16[64,32,8,512]{3,2,1,0:T(8,128)(2,1)} async-done(((bf16[64,32,8,512]{3,2,1,0:T(8,128)(2,1)}), bf16[64,32,8,512]{3,2,1,0:T(8,128)(2,1)}, u32[]{:S(2)}, u32[]{:S(2)}) %all-to-all-start) | async-done | bytes 16777248 | tf_op jit(solution)/shard_map/all_to_all | solution.py:53
  438.5 8.8 %fusion.29 = bf16[32,8,512]{2,1,0:T(8,128)(2,1)} fusion(bf16[32,8,512]{2,1,0:T(8,128)(2,1)S(1)} %bitcast.56, bf16[64,32,8,512]{3,2,1,0:T(8,128)(2,1)} %all-to-all-done), kind=kOutput, calls=%fused_computation.39 | convolution fusion | flops 134348800 | bytes 17301504 | tf_op jit(solution)/shard_map/cik,cjk->cij/dot_general | solution.py:23
  447.4 0.3 fusion.13
  447.7 40.7 %all-gather.5.cloned.1.call-done = bf16[128,8,512]{2,1,0:T(8,128)(2,1)} async-done(((bf16[32,8,512]{2,1,0:T(8,128)(2,1)}), bf16[128,8,512]{2,1,0:T(8,128)(2,1)}) %all-gather.5.cloned.1.call-update) | async-done | bytes 1048592 | tf_op jit(solution)/shard_map/all_gather | solution.py:57
  488.4 1.5 convert_reduce_fusion
  489.9 1.6 fusion.21
  491.5 0.4 fusion.24
  491.9 0.4 copy.23
  492.4 0.3 fusion.16
  492.6 0.1 copy.24
  492.7 0.8 copy.17
  493.6 0.1 bitcast_bitcast_fusion
  493.7 1.0 reshape.100
  494.7 25.8 %all_to_all.23 = bf16[64,2,1024]{2,1,0:T(2,128)(2,1)S(1)} all-to-all(bf16[64,2,1024]{2,1,0:T(2,128)(2,1)S(1)} %reshape.100), channel_id=1, replica_groups=mesh['row'=64,'ch'=4] {'row'}, dimensions={0} | all-to-all | bytes 524288 | tf_op jit(solution)/shard_map/all_to_all | solution.py:64
  520.5 0.5 reshape.101
  521.0 0.2 copy.32
  521.2 1.3 copy.19
  (30 shorter events, 0.1 us)
Async XLA Ops:
  6.5 34.1 %copy-start = (bf16[128,32]{0,1:T(8,128)(2,1)S(1)}, bf16[128,32]{0,1:T(8,128)(2,1)}, u32[]{:S(2)}) copy-start(bf16[128,32]{0,1:T(8,128)(2,1)} %param.17) | copy-start | bytes 24580
  6.5 33.2 %copy-start.6 = (f32[128]{0:T(128)S(1)}, f32[128]{0:T(128)}, u32[]{:S(2)}) copy-start(f32[128]{0:T(128)} %param.13) | copy-start | bytes 1540
  6.5 33.2 %copy-start.7 = (f32[128]{0:T(128)S(1)}, f32[128]{0:T(128)}, u32[]{:S(2)}) copy-start(f32[128]{0:T(128)} %param.12) | copy-start | bytes 1540
  6.5 30.1 %all-gather.3.cloned.1.call-start = ((), (), s32[]{:S(2)}) async-start(), calls=%async_computation.2 | async-start | bytes 1310720 | tf_op jit(solution)/shard_map/all_gather | solution.py:41
  36.7 3.1 copy-start.2
  40.2 0.7 copy-start.3
  47.3 12.8 %copy-start.10 = (bf16[128,32]{0,1:T(8,128)(2,1)S(1)}, bf16[128,32]{0,1:T(8,128)(2,1)}, u32[]{:S(2)}) copy-start(bf16[128,32]{0,1:T(8,128)(2,1)} %param.15) | copy-start | bytes 24580
  47.3 391.2 %all-to-all-start = ((bf16[64,32,8,512]{3,2,1,0:T(8,128)(2,1)}), bf16[64,32,8,512]{3,2,1,0:T(8,128)(2,1)}, u32[]{:S(2)}, u32[]{:S(2)}) async-start(bf16[64,32,8,512]{3,2,1,0:T(8,128)(2,1)} %stack.2), calls=%async_computation | async-start | bytes 33554432 | tf_op jit(solution)/shard_map/all_to_all | solution.py:53
  60.0 0.7 copy-start.4
  60.0 428.4 %all-gather.5.cloned.1.call-start = ((), (), s32[]{:S(2)}) async-start(), calls=%async_computation.3 | async-start | bytes 1310720 | tf_op jit(solution)/shard_map/all_gather | solution.py:57
  438.5 8.8 %copy-start.11 = (bf16[128,32]{0,1:T(8,128)(2,1)S(1)}, bf16[128,32]{0,1:T(8,128)(2,1)}, u32[]{:S(2)}) copy-start(bf16[128,32]{0,1:T(8,128)(2,1)} %param.18) | copy-start | bytes 24580
  447.3 44.2 %copy-start.8 = (f32[128]{0:T(128)S(1)}, f32[128]{0:T(128)}, u32[]{:S(2)}) copy-start(f32[128]{0:T(128)} %param.20) | copy-start | bytes 1540
  447.4 44.1 %copy-start.9 = (f32[128]{0:T(128)S(1)}, f32[128]{0:T(128)}, u32[]{:S(2)}) copy-start(f32[128]{0:T(128)} %param.19) | copy-start | bytes 1540
  488.4 3.1 copy-start.1
  491.5 0.8 copy-start.5
Sparse Core Ops, SparseCore 0:
  9.2 27.4 all-gather.2
  447.5 40.9 all-gather.4
